TPU v7x, 768 devices: a whole 4x8x12 slice. The times are simulated.
768 devices in a mesh: fsdp: 24 (over z, core), rep: 32 (over x, y).
Axes of the slice: x: 4, y: 8, z: 12, core: 2. Of those that a mesh axis runs over, the one named last changes fastest.
Arguments:
- grad_partial: bfloat16 [32, 144, 512, 512], P('rep', 'fsdp'), may hold values from -3 to 3
- basis_left: bfloat16 [144, 512, 512], P('fsdp'), may hold values from -0.25 to 0.25
- basis_right: bfloat16 [144, 512, 512], P('fsdp'), may hold values from -0.25 to 0.25
- owner_table: int32 [144], replicated, may hold values from 0 to 23, as said below
- moment_first: bfloat16 [24, 12, 512, 512], P('fsdp', None, 'rep'), may hold values from -6 to 6
- moment_second: float32 [24, 12, 512, 512], P('fsdp', None, 'rep'), may hold values from 0.1 to 10
Outputs:
- update: bfloat16 [144, 512, 512], P('fsdp', 'rep')
- new_first: bfloat16 [24, 12, 512, 512], P('fsdp', None, 'rep')
- new_second: float32 [24, 12, 512, 512], P('fsdp', None, 'rep')
Inputs may be any that keep to these rules, and one draw needn't show every extreme that they name: `owner_table`: block b belongs to the shard of fsdp index b // 6. At most 1 block of one shard name the same owner, and at most 12 blocks in all name the same owner; both bounds are reached in every draw.
All inputs are finite; a program needn't handle non-finite values.
Results may differ from a plain program's by a relative error of at most 0.015.
Values may be sent and summed in bfloat16 or wider, within the bound.
A program may use at most 64 MiB of HBM per device.

v0:
```python
import functools

import jax
import jax.numpy as jnp
from jax import lax
from jax.experimental import pallas as pl
from jax.experimental.pallas import tpu as pltpu
from jax.sharding import PartitionSpec as P

BETA_ONE = 0.9
BETA_TWO = 0.95
EPSILON = 1e-08
GRID_X = 4
LANES = 128
CHUNKS = 2
F32 = jnp.float32
BF16 = jnp.bfloat16


def kernel(
    sizes,
    grad_hbm,
    left_hbm,
    right_hbm,
    table,
    first_hbm,
    second_hbm,
    update,
    new_first,
    new_second,
    grad,
    left,
    right,
    first,
    second,
    total_back,
    part_a,
    part_b,
    ring_a_x,
    direct_a,
    ring_b_y,
    direct_b,
    reduced,
    outgoing,
    incoming,
    sendback,
    comeback,
    piece,
    gathered,
    product,
    rows_in,
    slot_table,
    in_sem,
    ring_send,
    ring_recv,
    swap_send,
    swap_recv,
):
    fsdp, nx, ny, chunks, width, blocks, slots = sizes
    rep = nx * ny
    cols = width // LANES
    half_blocks = blocks // 2
    units = blocks * cols
    shard = lax.axis_index("fsdp")
    replica = lax.axis_index("rep")
    my_x = replica // ny
    my_y = replica % ny

    def at_fsdp(step):
        return {"fsdp": (shard + step) % fsdp}

    def at_rep(step):
        return {"rep": (replica + step) % rep}

    def load(k, which):
        source, target = ((grad_hbm.at[0], grad), (left_hbm, left), (right_hbm, right))[which]
        return pltpu.make_async_copy(source.at[k], target.at[k], in_sem.at[which, k])

    def load_blocks(low, high):
        for k in range(low, high):
            for which in (0, 2, 1):
                load(k, which).start()

    load_blocks(half_blocks, blocks)
    barrier = pltpu.get_barrier_semaphore()

    def greet(axis):
        def body(step, carry):
            pl.semaphore_signal(
                barrier, inc=1, device_id=axis(step), device_id_type=pl.DeviceIdType.MESH
            )
            return carry

        return body

    lax.fori_loop(1, fsdp, greet(at_fsdp), 0)
    lax.fori_loop(1, rep, greet(at_rep), 0)
    load_first = pltpu.make_async_copy(first_hbm.at[0], first, in_sem.at[3, 0])
    load_second = pltpu.make_async_copy(second_hbm.at[0], second, in_sem.at[3, 1])
    load_first.start()
    load_second.start()
    load_blocks(0, half_blocks)

    def rotate(low, high):
        def body(k, carry):
            for which in (0, 2, 1):
                load(k, which).wait()
            right_part = jnp.dot(grad[k], right[k], preferred_element_type=F32)
            rotated = lax.dot_general(
                left[k],
                right_part.astype(BF16),
                (((0,), (0,)), ((), ())),
                preferred_element_type=F32,
            ).astype(BF16)
            for q in range(chunks):
                rows = rotated[:, q * width : (q + 1) * width].reshape(nx, ny, 16, width)
                if low == 0:
                    for x in range(nx):
                        part_a[q, x, k] = rows[x]
                else:
                    for y in range(ny):
                        part_b[q, y, k - low] = rows[:, y]
            return carry

        lax.fori_loop(low, high, body, 0)

    def remote(source, target, send, recv, device):
        return pltpu.make_async_remote_copy(
            src_ref=source,
            dst_ref=target,
            send_sem=send,
            recv_sem=recv,
            device_id=device,
            device_id_type=pl.DeviceIdType.MESH,
        )

    sent = []

    def ring(count, position, piece, landing, sems, device):
        reach = count // 2
        flying = {}

        def copy(way, step):
            there = (position + way * (reach - step + 1) + count) % count
            side = 0 if way > 0 else 1
            cut = None if step > 1 else side
            return remote(
                piece(there, cut),
                landing(side, step - 1, cut),
                ring_send.at[sems + (side, step - 1)],
                ring_recv.at[sems + (side, step - 1)],
                device(way),
            )

        for step in range(1, reach + 1):
            for way in (1, -1):
                side = 0 if way > 0 else 1
                if step > 1:
                    flying[way].wait_recv()
                    there = (position + way * (reach - step + 1) + count) % count
                    cut = side if step == 2 else None
                    held = piece(there, cut)
                    held[...] = held[...] + landing(side, step - 2, cut)[...]
                flying[way] = copy(way, step)
                flying[way].start()
                sent.append(flying[way])
            yield
        flying[1].wait_recv()
        flying[-1].wait_recv()

    def split(low, count, cut):
        if cut is None:
            return pl.ds(low, count)
        middle = (count + 1) // 2
        return pl.ds(low, middle) if cut == 0 else pl.ds(low + middle, count - middle)

    def along_x(way):
        return {"rep": ((my_x + way + nx) % nx) * ny + my_y}

    def along_y(way):
        return {"rep": my_x * ny + (my_y + way + ny) % ny}

    def total(own, landed):
        result = own.astype(F32)
        for value in landed:
            result = result + value.astype(F32)
        return result

    def direct(count, piece, landing, sems, device):
        for step in sorted(range(1, count), key=lambda step: -min(step, count - step)):
            remote(
                piece(step),
                landing.at[step],
                swap_send.at[sems],
                swap_recv.at[sems],
                device(step),
            ).start()
        others = landing.at[pl.ds(1, count - 1)]
        whole = remote(others, others, swap_send.at[sems], swap_recv.at[sems], device(1))
        sent.append(whole)
        return whole

    def sum_a(q):
        yield from ring(
            nx,
            my_x,
            lambda there, cut: part_a.at[q, there, :, split(0, ny, cut)],
            lambda side, step, cut: ring_a_x.at[q, side, step, :, split(0, ny, cut)],
            (q, 0),
            along_x,
        )
        for k in range(half_blocks):
            part_a[q, my_x, k] = total(
                part_a[q, my_x, k], [ring_a_x[q, side, nx // 2 - 1, k] for side in (0, 1)]
            ).astype(BF16)
        whole = direct(
            ny,
            lambda step: part_a.at[q, my_x, :, (my_y + step) % ny],
            direct_a.at[q],
            (q, 4),
            along_y,
        )
        yield
        whole.wait_recv()
        for k in range(half_blocks):
            reduced[q, k] = total(
                part_a[q, my_x, k, my_y], [direct_a[q, step, k] for step in range(1, ny)]
            ).astype(BF16)

    def sum_b(q):
        yield from ring(
            ny,
            my_y,
            lambda there, cut: part_b.at[q, there, :, split(0, nx, cut)],
            lambda side, step, cut: ring_b_y.at[q, side, step, :, split(0, nx, cut)],
            (q, 1),
            along_y,
        )
        for k in range(blocks - half_blocks):
            part_b[q, my_y, k] = total(
                part_b[q, my_y, k],
                [ring_b_y[q, side, ny // 2 - 1, k] for side in (0, 1)],
            ).astype(BF16)
        whole = direct(
            nx,
            lambda step: part_b.at[q, my_y, :, (my_x + step) % nx],
            direct_b.at[q],
            (q, 5),
            along_x,
        )
        yield
        whole.wait_recv()
        for k in range(blocks - half_blocks):
            reduced[q, half_blocks + k] = total(
                part_b[q, my_y, k, my_x],
                [direct_b[q, step, k] for step in range(1, nx)],
            ).astype(BF16)

    def ranks():
        def of_shard(other, rank):
            slot_table[other] = rank
            for k in range(blocks):
                rank += (table[other * blocks + k] == shard).astype(jnp.int32)
            return rank

        slot_table[2 * fsdp + slots] = lax.fori_loop(0, fsdp, of_shard, jnp.int32(0))

    def lookups():
        def of_shard(other, picks):
            rank = slot_table[other]
            away = (shard - other + fsdp) % fsdp
            return tuple(jnp.where(rank == j, away, picks[j]) for j in range(slots))

        picks = lax.fori_loop(0, fsdp, of_shard, (jnp.int32(0),) * slots)
        for j in range(slots):
            slot_table[2 * fsdp + j] = picks[j]

        def of_owner(owner, carry):
            block = jnp.int32(0)
            for k in range(blocks):
                block = jnp.where(table[shard * blocks + k] == owner, k, block)
            slot_table[fsdp + owner] = block
            return carry

        lax.fori_loop(0, fsdp, of_owner, 0)

    def swap(q, which, source, target, fill):
        def start(turn, carry):
            pair = turn // 2
            across = fsdp // 4 + jnp.where(pair % 2 == 0, pair // 2, -(pair + 1) // 2)
            step = 2 * across + 1 - turn % 2
            fill(source.at[step], (shard + step) % fsdp)
            remote(
                source.at[step],
                target.at[step],
                swap_send.at[q, which],
                swap_recv.at[q, which],
                at_fsdp(step),
            ).start()
            return carry

        lax.fori_loop(0, fsdp - 1, start, 0)
        fill(target.at[0], shard)
        others = pl.ds(1, fsdp - 1)
        whole = remote(
            source.at[others],
            target.at[others],
            swap_send.at[q, which],
            swap_recv.at[q, which],
            at_fsdp(1),
        )
        sent.append(whole)
        return whole

    def to_owners(q):
        def fill(slot, owner):
            slot[...] = reduced[q, slot_table[fsdp + owner]]

        return swap(q, 0, outgoing[q], incoming[q], fill)

    def to_shards(q):
        columns = pl.ds(q * width, width)

        def fill(slot, other):
            held = jnp.minimum(slot_table[other], slots - 1)
            slot[0] = first[held, :, columns]
            slot[1] = second[held, :, columns].astype(BF16)

        return swap(q, 1, sendback[q], comeback[q], fill)

    def advanced(first_old, second_old, gradient):
        first_now = BETA_ONE * first_old + (1.0 - BETA_ONE) * gradient
        second_now = BETA_TWO * second_old + (1.0 - BETA_TWO) * gradient * gradient
        return first_now, second_now

    def keep_moments(q):
        columns = pl.ds(q * width, width)
        count = slot_table[2 * fsdp + slots]

        def body(j, carry):
            gradient = incoming[q][slot_table[2 * fsdp + j]].astype(F32)
            first_old = first[j, :, columns].astype(F32)
            second_old = second[j, :, columns]
            first_now, second_now = advanced(first_old, second_old, gradient)
            used = j < count
            new_first[0, j, :, columns] = jnp.where(used, first_now, first_old).astype(BF16)
            new_second[0, j, :, columns] = jnp.where(used, second_now, second_old)
            return carry

        lax.fori_loop(0, slots, body, 0)

    def to_units(q):
        base = q * units

        for k in range(blocks):
            away = (shard - table[shard * blocks + k] + fsdp) % fsdp
            first_now, second_now = advanced(
                comeback[q][away, 0].astype(F32),
                comeback[q][away, 1].astype(F32),
                reduced[q, k].astype(F32),
            )
            rows = (first_now / (jnp.sqrt(second_now) + EPSILON)).astype(BF16)
            for c in range(cols):
                piece[base + k * cols + c] = rows[:, c * LANES : (c + 1) * LANES]

        def start(unit, carry):
            @pl.when(unit != replica)
            def _():
                remote(
                    piece.at[unit],
                    gathered.at[replica],
                    swap_send.at[q, 2],
                    swap_recv.at[q, 2],
                    {"rep": unit},
                ).start()

            @pl.when(unit == replica)
            def _():
                gathered[unit] = piece[unit]

            return carry

        lax.fori_loop(base, base + units, start, 0)

    def unit_copy(q, count):
        return remote(
            gathered.at[pl.ds(0, count)],
            gathered.at[pl.ds(0, count)],
            swap_send.at[q, 2],
            swap_recv.at[q, 2],
            at_rep(1),
        )

    def row_copy(q, count):
        return remote(
            product.at[pl.ds(0, count)],
            product.at[pl.ds(0, count)],
            swap_send.at[q, 3],
            swap_recv.at[q, 3],
            at_rep(1),
        )

    def is_unit(q):
        return (replica >= q * units) & (replica < (q + 1) * units)

    def rotate_left(q):
        @pl.when(is_unit(q))
        def _():
            unit_copy(q, rep - 1).wait_recv()
            block = (replica - q * units) // cols
            back = jnp.dot(
                left[block],
                gathered[...].reshape(rep * 16, LANES),
                preferred_element_type=F32,
            )
            product[...] = back.astype(BF16).reshape(rep, 16, LANES)

            def start(step, carry):
                other = (replica + step) % rep
                remote(
                    product.at[other],
                    rows_in.at[replica],
                    swap_send.at[q, 3],
                    swap_recv.at[q, 3],
                    {"rep": other},
                ).start()
                return carry

            lax.fori_loop(1, rep, start, 0)
            rows_in[replica] = product[replica]

    def finish(q):
        @pl.when(is_unit(q))
        def _():
            row_copy(q, units - 1).wait_recv()

        @pl.when(jnp.logical_not(is_unit(q)))
        def _():
            row_copy(q, units).wait_recv()

        base = q * units
        for k in range(blocks):
            rows = jnp.concatenate([rows_in[base + k * cols + c] for c in range(cols)], axis=1)
            back = lax.dot_general(
                rows,
                right[k, :, q * width : (q + 1) * width],
                (((1,), (1,)), ((), ())),
                preferred_element_type=F32,
            )
            if q > 0:
                back = back + total_back[k]
            if q < chunks - 1:
                total_back[k] = back
            else:
                update[k] = back.astype(BF16)

    scope = jax.named_scope
    each = range(chunks)
    with scope("rotate_b"):
        rotate(half_blocks, blocks)
    with scope("greeting"):
        pl.semaphore_wait(barrier, fsdp + rep - 2)
    b = [sum_b(q) for q in each]
    for q in each:
        next(b[q])
    with scope("ranks"):
        ranks()
        load_first.wait()
        load_second.wait()
    with scope("to_shards0"):
        moments = [to_shards(0)]
    with scope("rotate_a"):
        rotate(0, half_blocks)
    a = [sum_a(q) for q in each]
    for q in each:
        next(a[q])
    turns = {}

    def go(*names):
        for name in names:
            turns[name] = turns.get(name, 1) + 1
            with scope(f"{name}_turn{turns[name]}"):
                next((a if name[0] == "a" else b)[int(name[1])], None)

    go("b0", "b1")
    for q in range(1, chunks):
        with scope(f"to_shards{q}"):
            moments.append(to_shards(q))
    go("a0", "b0", "a1", "b1")
    with scope("lookups"):
        lookups()
    go("b0", "b1", "a0", "a1", "b0", "b1")
    arrivals = []
    for q in each:
        go(f"a{q}", f"b{q}")
        with scope(f"wait_moments{q}"):
            moments[q].wait_recv()
        with scope(f"to_units{q}"):
            to_units(q)
        with scope(f"to_owners{q}"):
            arrivals.append(to_owners(q))
    for q in each:
        with scope(f"rotate_left{q}"):
            rotate_left(q)
    for q in each:
        with scope(f"wait_owners{q}"):
            arrivals[q].wait_recv()
        with scope(f"keep_moments{q}"):
            keep_moments(q)
        if q < chunks - 1:
            with scope(f"finish{q}"):
                finish(q)

    with scope("sent"):
        for copy in sent:
            copy.wait_send()
    with scope(f"finish{chunks - 1}"):
        finish(chunks - 1)
    for q in each:

        @pl.when(is_unit(q))
        def _(q=q):
            unit_copy(q, units - 1).wait_send()
            row_copy(q, rep - 1).wait_send()

        @pl.when(jnp.logical_not(is_unit(q)))
        def _(q=q):
            unit_copy(q, units).wait_send()


def copy_kernel(*refs):
    count = len(refs) // 2
    sources, targets, sems = refs[:count], refs[count : 2 * count], refs[-1]
    copies = [
        pltpu.make_async_copy(source, target, sems.at[i])
        for i, (source, target) in enumerate(zip(sources, targets))
    ]
    for copy in copies:
        copy.start()
    for copy in copies:
        copy.wait()


def body(grad_partial, basis_left, basis_right, owner_table, moment_first, moment_second):
    fsdp = lax.axis_size("fsdp")
    rep = lax.axis_size("rep")
    blocks, size = basis_left.shape[0], basis_left.shape[1]
    slots, rows = moment_first.shape[1], moment_first.shape[2]
    nx = GRID_X
    ny = rep // nx
    width = size // CHUNKS
    half = blocks // 2
    cols = width // LANES
    sizes = (fsdp, nx, ny, CHUNKS, width, blocks, slots)
    anywhere = pl.BlockSpec(memory_space=pl.ANY)

    def vmem(*shape, kind=BF16):
        return pltpu.VMEM(shape, kind)

    tile = (rows, width)
    scratch = [
        vmem(blocks, size, size),
        vmem(blocks, size, size),
        vmem(blocks, size, size),
        vmem(slots, rows, size),
        vmem(slots, rows, size, kind=F32),
        vmem(blocks, rows, size, kind=F32),
        vmem(CHUNKS, nx, half, ny, *tile),
        vmem(CHUNKS, ny, blocks - half, nx, *tile),
        vmem(CHUNKS, 2, nx // 2, half, ny, *tile),
        vmem(CHUNKS, ny, half, *tile),
        vmem(CHUNKS, 2, ny // 2, blocks - half, nx, *tile),
        vmem(CHUNKS, nx, blocks - half, *tile),
        vmem(CHUNKS, blocks, *tile),
        [vmem(fsdp, *tile) for _ in range(CHUNKS)],
        [vmem(fsdp, *tile) for _ in range(CHUNKS)],
        [vmem(fsdp, 2, *tile) for _ in range(CHUNKS)],
        [vmem(fsdp, 2, *tile) for _ in range(CHUNKS)],
        vmem(CHUNKS * blocks * cols, rows, LANES),
        vmem(rep, rows, LANES),
        vmem(rep, rows, LANES),
        vmem(CHUNKS * blocks * cols, rows, LANES),
        pltpu.SMEM((2 * fsdp + slots + 1,), jnp.int32),
        pltpu.SemaphoreType.DMA((4, blocks)),
        pltpu.SemaphoreType.DMA((CHUNKS, 2, 2, ny // 2)),
        pltpu.SemaphoreType.DMA((CHUNKS, 2, 2, ny // 2)),
        pltpu.SemaphoreType.DMA((CHUNKS, 6)),
        pltpu.SemaphoreType.DMA((CHUNKS, 6)),
    ]
    results = pl.pallas_call(
        functools.partial(kernel, sizes),
        out_shape=(
            pltpu.VMEM((blocks, rows, size), BF16),
            pltpu.VMEM(moment_first.shape, BF16),
            pltpu.VMEM(moment_second.shape, F32),
        ),
        in_specs=[
            anywhere,
            anywhere,
            anywhere,
            pl.BlockSpec(memory_space=pltpu.SMEM),
            anywhere,
            anywhere,
        ],
        out_specs=(pl.BlockSpec(memory_space=pltpu.VMEM),) * 3,
        scratch_shapes=scratch,
        compiler_params=pltpu.CompilerParams(
            collective_id=0, has_side_effects=True, vmem_limit_bytes=56 * 1024 * 1024
        ),
    )(grad_partial, basis_left, basis_right, owner_table, moment_first, moment_second)
    return pl.pallas_call(
        copy_kernel,
        out_shape=tuple(jax.ShapeDtypeStruct(r.shape, r.dtype) for r in results),
        in_specs=[pl.BlockSpec(memory_space=pltpu.VMEM)] * 3,
        out_specs=(pl.BlockSpec(memory_space=pltpu.HBM),) * 3,
        scratch_shapes=[pltpu.SemaphoreType.DMA((3,))],
    )(*[pltpu.with_memory_space_constraint(r, pltpu.VMEM) for r in results])


def solution(mesh):
    placed = (
        P("rep", "fsdp", None, None),
        P("fsdp", None, None),
        P("fsdp", None, None),
        P(),
        P("fsdp", None, "rep", None),
        P("fsdp", None, "rep", None),
    )
    return jax.shard_map(
        body,
        mesh=mesh,
        in_specs=placed,
        out_specs=(
            P("fsdp", "rep", None),
            P("fsdp", None, "rep", None),
            P("fsdp", None, "rep", None),
        ),
        check_vma=False,
    )
```

profile of v0, /device:TPU:1, one launch (start us, length us, event | category | flops | bytes accessed | tf_op | source)
XLA Modules:
  0.0 65.7 jit_solution(2120348806119325259)
XLA Ops:
  0.6 64.2 %shard_map.85 = (bf16[6,16,512]{2,1,0:T(8,128)(2,1)S(1)}, bf16[1,12,16,512]{3,2,1,0:T(8,128)(2,1)S(1)}, f32[1,12,16,512]{3,2,1,0:T(8,128)S(1)}) custom-call(bf16[1,6,512,512]{3,2,1,0:T(8,128)(2,1)} %grad_hbm.1, bf16[6,512,512]{2,1,0:T(8,128)(2,1)} %left_hbm.1, bf16[6,512,512]{2,1,0:T(8,128)(2,1)} %right_hbm.1, s32[144]{0:T(256)} %table.1, ...), custom_call_target="tpu_custom_call" | custom-call | tf_op jit(solution)/shard_map/pallas_call | solution.py:590
  64.8 0.9 %shard_map.86 = (bf16[6,16,512]{2,1,0:T(8,128)(2,1)}, bf16[1,12,16,512]{3,2,1,0:T(8,128)(2,1)}, f32[1,12,16,512]{3,2,1,0:T(8,128)}) custom-call(bf16[6,16,512]{2,1,0:T(8,128)(2,1)S(1)} %get-tuple-element.6.refs_0_, bf16[1,12,16,512]{3,2,1,0:T(8,128)(2,1)S(1)} %get-tuple-element.7.refs_1_, f32[1,12,16,512]{3,2,1,0:T(8,128)S(1)} %get-tuple-element.8.refs_2_), custom_call_target="tpu_custom_call" | custom-call | tf_op jit(solution)/shard_map/pallas_call | solution.py:611
where the time goes:
time: 65.8 us; the launch traced here: 65.7 us
  Pallas kernels  65 us (99%)
    pallas_call x1, Pallas kernels, body(): pl.pallas_call(functools.partial(kernel, sizes), out_shape=(pltpu.VMEM((b...  64.2 us

commit v1 on v0

--- a/solution.py
+++ b/solution.py
@@ -487,35 +487,38 @@
         with scope(f"to_shards{q}"):
             moments.append(to_shards(q))
     go("a0", "b0", "a1", "b1")
+    go("b0", "b1", "a0", "a1", "b0", "b1")
     with scope("lookups"):
         lookups()
-    go("b0", "b1", "a0", "a1", "b0", "b1")
     arrivals = []
     for q in each:
         go(f"a{q}", f"b{q}")
+        if q < chunks - 1:
+            with scope(f"to_owners{q}"):
+                arrivals.append(to_owners(q))
         with scope(f"wait_moments{q}"):
             moments[q].wait_recv()
         with scope(f"to_units{q}"):
             to_units(q)
-        with scope(f"to_owners{q}"):
-            arrivals.append(to_owners(q))
+        if q == chunks - 1:
+            with scope(f"to_owners{q}"):
+                arrivals.append(to_owners(q))
     for q in each:
         with scope(f"rotate_left{q}"):
             rotate_left(q)
     for q in each:
+        if q == chunks - 1:
+            for earlier in each:
+                with scope(f"finish{earlier}"):
+                    finish(earlier)
         with scope(f"wait_owners{q}"):
             arrivals[q].wait_recv()
         with scope(f"keep_moments{q}"):
             keep_moments(q)
-        if q < chunks - 1:
-            with scope(f"finish{q}"):
-                finish(q)
 
     with scope("sent"):
         for copy in sent:
             copy.wait_send()
-    with scope(f"finish{chunks - 1}"):
-        finish(chunks - 1)
     for q in each:
 
         @pl.when(is_unit(q))

time: 65.8 us -> 65.7 us (level)
  no operation moved by 1% of the time
where the time goes in v1:
time: 65.7 us; the launch traced here: 65.1 us
  Pallas kernels  64.5 us (98%)
    pallas_call x1, Pallas kernels, body(): pl.pallas_call(functools.partial(kernel, sizes), out_shape=(pltpu.VMEM((b...  63.6 us

profile of v1, /device:TPU:1, one launch (start us, length us, event | category | flops | bytes accessed | tf_op | source)
XLA Modules:
  0.0 65.1 jit_solution(5818241024830938197)
XLA Ops:
  0.6 63.6 %shard_map.85 = (bf16[6,16,512]{2,1,0:T(8,128)(2,1)S(1)}, bf16[1,12,16,512]{3,2,1,0:T(8,128)(2,1)S(1)}, f32[1,12,16,512]{3,2,1,0:T(8,128)S(1)}) custom-call(bf16[1,6,512,512]{3,2,1,0:T(8,128)(2,1)} %grad_hbm.1, bf16[6,512,512]{2,1,0:T(8,128)(2,1)} %left_hbm.1, bf16[6,512,512]{2,1,0:T(8,128)(2,1)} %right_hbm.1, s32[144]{0:T(256)} %table.1, ...), custom_call_target="tpu_custom_call" | custom-call | tf_op jit(solution)/shard_map/pallas_call | solution.py:593
  64.3 0.9 %shard_map.86 = (bf16[6,16,512]{2,1,0:T(8,128)(2,1)}, bf16[1,12,16,512]{3,2,1,0:T(8,128)(2,1)}, f32[1,12,16,512]{3,2,1,0:T(8,128)}) custom-call(bf16[6,16,512]{2,1,0:T(8,128)(2,1)S(1)} %get-tuple-element.6.refs_0_, bf16[1,12,16,512]{3,2,1,0:T(8,128)(2,1)S(1)} %get-tuple-element.7.refs_1_, f32[1,12,16,512]{3,2,1,0:T(8,128)S(1)} %get-tuple-element.8.refs_2_), custom_call_target="tpu_custom_call" | custom-call | tf_op jit(solution)/shard_map/pallas_call | solution.py:614

commit v2 on v1

--- a/solution.py
+++ b/solution.py
@@ -66,11 +66,14 @@
     my_x = replica // ny
     my_y = replica % ny
 
+    def wrap(value, count):
+        return jnp.where(value >= count, value - count, value)
+
     def at_fsdp(step):
-        return {"fsdp": (shard + step) % fsdp}
+        return {"fsdp": wrap(shard + step, fsdp)}
 
     def at_rep(step):
-        return {"rep": (replica + step) % rep}
+        return {"rep": wrap(replica + step, rep)}
 
     def load(k, which):
         source, target = ((grad_hbm.at[0], grad), (left_hbm, left), (right_hbm, right))[which]
@@ -93,13 +96,12 @@
 
         return body
 
-    lax.fori_loop(1, fsdp, greet(at_fsdp), 0)
-    lax.fori_loop(1, rep, greet(at_rep), 0)
+    lax.fori_loop(1, fsdp, greet(at_fsdp), 0, unroll=True)
+    lax.fori_loop(1, rep, greet(at_rep), 0, unroll=True)
     load_first = pltpu.make_async_copy(first_hbm.at[0], first, in_sem.at[3, 0])
     load_second = pltpu.make_async_copy(second_hbm.at[0], second, in_sem.at[3, 1])
     load_first.start()
     load_second.start()
-    load_blocks(0, half_blocks)
 
     def rotate(low, high):
         def body(k, carry):
@@ -289,7 +291,7 @@
             pair = turn // 2
             across = fsdp // 4 + jnp.where(pair % 2 == 0, pair // 2, -(pair + 1) // 2)
             step = 2 * across + 1 - turn % 2
-            fill(source.at[step], (shard + step) % fsdp)
+            fill(source.at[step], wrap(shard + step, fsdp))
             remote(
                 source.at[step],
                 target.at[step],
@@ -299,7 +301,7 @@
             ).start()
             return carry
 
-        lax.fori_loop(0, fsdp - 1, start, 0)
+        lax.fori_loop(0, fsdp - 1, start, 0, unroll=True)
         fill(target.at[0], shard)
         others = pl.ds(1, fsdp - 1)
         whole = remote(
@@ -416,7 +418,7 @@
             product[...] = back.astype(BF16).reshape(rep, 16, LANES)
 
             def start(step, carry):
-                other = (replica + step) % rep
+                other = wrap(replica + step, rep)
                 remote(
                     product.at[other],
                     rows_in.at[replica],
@@ -463,6 +465,7 @@
     b = [sum_b(q) for q in each]
     for q in each:
         next(b[q])
+    load_blocks(0, half_blocks)
     with scope("ranks"):
         ranks()
         load_first.wait()

time: 65.7 us -> 65.3 us (level)
  no operation moved by 1% of the time
where the time goes in v2:
time: 65.3 us; the launch traced here: 64.8 us
  Pallas kernels  64.1 us (98%)
    pallas_call x1, Pallas kernels, body(): pl.pallas_call(functools.partial(kernel, sizes), out_shape=(pltpu.VMEM((b...  63.2 us

profile of v2, /device:TPU:1, one launch (start us, length us, event | category | flops | bytes accessed | tf_op | source)
XLA Modules:
  0.0 64.8 jit_solution(5646058592715560891)
XLA Ops:
  0.6 63.2 %shard_map.85 = (bf16[6,16,512]{2,1,0:T(8,128)(2,1)S(1)}, bf16[1,12,16,512]{3,2,1,0:T(8,128)(2,1)S(1)}, f32[1,12,16,512]{3,2,1,0:T(8,128)S(1)}) custom-call(bf16[1,6,512,512]{3,2,1,0:T(8,128)(2,1)} %grad_hbm.1, bf16[6,512,512]{2,1,0:T(8,128)(2,1)} %left_hbm.1, bf16[6,512,512]{2,1,0:T(8,128)(2,1)} %right_hbm.1, s32[144]{0:T(256)} %table.1, ...), custom_call_target="tpu_custom_call" | custom-call | tf_op jit(solution)/shard_map/pallas_call | solution.py:596
  63.9 0.9 %shard_map.86 = (bf16[6,16,512]{2,1,0:T(8,128)(2,1)}, bf16[1,12,16,512]{3,2,1,0:T(8,128)(2,1)}, f32[1,12,16,512]{3,2,1,0:T(8,128)}) custom-call(bf16[6,16,512]{2,1,0:T(8,128)(2,1)S(1)} %get-tuple-element.6.refs_0_, bf16[1,12,16,512]{3,2,1,0:T(8,128)(2,1)S(1)} %get-tuple-element.7.refs_1_, f32[1,12,16,512]{3,2,1,0:T(8,128)S(1)} %get-tuple-element.8.refs_2_), custom_call_target="tpu_custom_call" | custom-call | tf_op jit(solution)/shard_map/pallas_call | solution.py:617
